TPU v7x, 32 devices: a whole 2x2x4 slice. The times are simulated.
32 devices in a mesh: mode: 4 (over z), gx: 4 (over x, core), gy: 2 (over y).
Axes of the slice: x: 2, y: 2, z: 4, core: 2. Of those that a mesh axis runs over, the one named last changes fastest.
Arguments:
- values: float32 [8, 40, 160, 8, 128], P('mode', 'gx', 'gy'), may hold values from -6 to 6
- coef_table: float32 [3, 4], replicated, may hold values from -1 to 1
- mode_coef: int32 [8], P('mode'), may hold values from 0 to 3
- switch_mask: int32 [8, 8], replicated, may hold values 0 or 1
- switch_cost: float32 [8, 8], replicated, may hold values from 0 to 1
Outputs:
- sectioned: float32 [8, 40, 160, 2, 128], P('mode', 'gx', 'gy')
All inputs are finite; a program needn't handle non-finite values.
Results may differ from a plain program's by a relative error of at most 0.0003.
Values sent between devices are 32-bit elements; how exact they have to be, the bound alone decides.
A program may use at most 128 MiB of HBM per device.

v0:
```python
import jax
import jax.numpy as jnp
from jax import lax
from jax.sharding import PartitionSpec as P

epsilon = 1e-06
time_step = 0.1


def extended_2(cells, sides, width):
    for axis, dim in sides:
        count = lax.axis_size(axis)
        ends = count - 1
        head = lax.slice_in_dim(cells, 0, width, axis=dim)
        tail = lax.slice_in_dim(cells, cells.shape[dim] - width, cells.shape[dim], axis=dim)
        cells = jnp.concatenate(
            [
                lax.ppermute(tail, axis, [(i, (i + 1) % count) for i in range(ends)]),
                cells,
                lax.ppermute(head, axis, [((i + 1) % count, i) for i in range(ends)]),
            ],
            axis=dim,
        )
    return cells


def weno_mix(d_one, d_two, d_three, d_four, d_five):
    smooth_one = (
        13.0 / 12.0 * (d_one - 2.0 * d_two + d_three) ** 2
        + 0.25 * (d_one - 4.0 * d_two + 3.0 * d_three) ** 2
    )
    smooth_two = 13.0 / 12.0 * (d_two - 2.0 * d_three + d_four) ** 2 + 0.25 * (d_two - d_four) ** 2
    smooth_three = (
        13.0 / 12.0 * (d_three - 2.0 * d_four + d_five) ** 2
        + 0.25 * (3.0 * d_three - 4.0 * d_four + d_five) ** 2
    )
    weight_one = 0.1 / (epsilon + smooth_one) ** 2
    weight_two = 0.6 / (epsilon + smooth_two) ** 2
    weight_three = 0.3 / (epsilon + smooth_three) ** 2
    weight_sum = weight_one + weight_two + weight_three
    mixed = weight_one * (d_one / 3.0 - 7.0 * d_two / 6.0 + 11.0 * d_three / 6.0)
    mixed = mixed + weight_two * (-d_two / 6.0 + 5.0 * d_three / 6.0 + d_four / 3.0)
    mixed = mixed + weight_three * (d_three / 3.0 + 5.0 * d_four / 6.0 - d_five / 6.0)
    return mixed / weight_sum


def weno_pair(extended, axis_no, length):
    spread = lax.slice_in_dim(extended, 1, length + 6, axis=axis_no) - lax.slice_in_dim(
        extended, 0, length + 5, axis=axis_no
    )
    shifted = [lax.slice_in_dim(spread, k, k + length, axis=axis_no) for k in range(6)]
    minus_side = weno_mix(shifted[0], shifted[1], shifted[2], shifted[3], shifted[4])
    plus_side = weno_mix(shifted[5], shifted[4], shifted[3], shifted[2], shifted[1])
    return (minus_side, plus_side)


def section_update(centre, slopes, shift_c, turn_raw, accel_c):
    heading = (
        2.0
        * jnp.pi
        * lax.broadcasted_iota(jnp.float32, centre.shape, centre.ndim - 1)
        / centre.shape[-1]
    )
    speed_value = 1.0 + 0.5 * lax.broadcasted_iota(jnp.float32, centre.shape, centre.ndim - 2)
    top_speed = 1.0 + 0.5 * (centre.shape[-2] - 1)
    turn_c = 0.5 + jnp.abs(turn_raw)
    means = [0.5 * (slopes[k][0] + slopes[k][1]) for k in range(4)]
    jumps = [slopes[k][1] - slopes[k][0] for k in range(4)]
    hamiltonian = means[0] * (speed_value * jnp.cos(heading) - shift_c) + means[
        1
    ] * speed_value * jnp.sin(heading)
    hamiltonian = hamiltonian + turn_c * jnp.abs(means[2]) + accel_c * means[3]
    dissipation = (
        (top_speed + jnp.abs(shift_c)) * jumps[0]
        + top_speed * jumps[1]
        + turn_c * jumps[2]
        + jnp.abs(accel_c) * jumps[3]
    )
    return centre - time_step * (hamiltonian - 0.5 * dissipation)


def shards(values, coef_table, mode_coef, switch_mask, switch_cost):
    mode_dev = values.shape[0]
    planes = values.shape[3] - 6
    centre = values[:, :, :, 3 : 3 + planes]
    joined = extended_2(centre, (("gx", 1), ("gy", 2)), 3)
    wide_one = joined[:, :, 3:-3]
    wide_two = joined[:, 3:-3]
    wide_three = jnp.concatenate([centre[..., -3:], centre, centre[..., :3]], axis=4)
    slopes = [
        weno_pair(wide_one, 1, centre.shape[1]),
        weno_pair(wide_two, 2, centre.shape[2]),
        weno_pair(wide_three, 4, centre.shape[4]),
        weno_pair(values, 3, planes),
    ]
    kind_count = coef_table.shape[1]
    onehot = mode_coef[:, None] == jnp.arange(kind_count, dtype=jnp.int32)[None, :]
    picked = jnp.sum(jnp.where(onehot[None], coef_table[:, None, :], 0.0), axis=2)
    column_shape = (mode_dev, 1, 1, 1, 1)
    updated = section_update(
        centre,
        slopes,
        picked[0].reshape(column_shape),
        picked[1].reshape(column_shape),
        picked[2].reshape(column_shape),
    )
    group_index = lax.axis_index("mode")
    own_modes = group_index * mode_dev + jnp.arange(mode_dev, dtype=jnp.int32)
    mask_rows = lax.dynamic_slice_in_dim(switch_mask, group_index * mode_dev, mode_dev, 0)
    cost_rows = lax.dynamic_slice_in_dim(switch_cost, group_index * mode_dev, mode_dev, 0)
    running = updated
    shard_piece = lax.all_gather(updated, "mode", axis=0, tiled=True)
    offset = jnp.int32(0)
    for k in range(shard_piece.shape[0]):
        source = offset + k
        allowed = (lax.dynamic_index_in_dim(mask_rows, source, 1, False) == 1) & (
            own_modes != source
        )
        cost_here = lax.dynamic_index_in_dim(cost_rows, source, 1, False)
        candidate = shard_piece[k][None] + cost_here.reshape(column_shape)
        running = jnp.where(allowed.reshape(column_shape), jnp.minimum(running, candidate), running)
    return running


def solution(mesh):
    in_specs = (P("mode", "gx", "gy", None, None), P(), P("mode"), P(), P())
    out_specs = P("mode", "gx", "gy", None, None)
    return jax.shard_map(shards, mesh=mesh, in_specs=in_specs, out_specs=out_specs, check_vma=False)
```

profile of v0, /device:TPU:0, one launch (start us, length us, event | category | flops | bytes accessed | tf_op | source)
XLA Modules:
  0.0 230.7 jit_solution(15683989817009822951)
XLA Ops:
  6.5 0.0 copy-start
  6.5 0.0 all-gather.2.cloned.1.call-start
  6.5 2.7 %fusion.2 = (f32[2,3,80,2,128]{4,3,2,1,0:T(2,128)S(1)}, f32[2,3,80,2,128]{4,3,2,1,0:T(2,128)S(1)}) fusion(f32[2,10,80,8,128]{4,3,2,1,0:T(8,128)} %param.5), kind=kLoop, calls=%fused_computation.65 | loop fusion | bytes 1966080 | tf_op jit(solution)/shard_map/slice | solution.py:14
  9.2 0.8 copy.23
  10.0 3.1 %collective-permute-start = (f32[2,3,80,2,128]{4,2,3,1,0:T(8,128)}, f32[2,3,80,2,128]{4,2,3,1,0:T(8,128)}, u32[]{:S(2)}, u32[]{:S(2)}) collective-permute-start(f32[2,3,80,2,128]{4,2,3,1,0:T(8,128)} %copy.23), channel_id=1, source_target_pairs={{0,2},{2,4},{4,6},{1,3},{3,5},{5,7},{8,10},{10,12},{12,14},{9,11},... | collective-permute-start | bytes 1474568 | tf_op jit(solution)/shard_map/ppermute | solution.py:18
  13.2 0.8 copy.24
  14.0 1.3 collective-permute-start.1
  15.3 11.3 %fusion.4 = (f32[2,10,80,7,128]{4,3,2,1,0:T(8,128)}, f32[2,10,80,7,128]{4,3,2,1,0:T(8,128)}) fusion(f32[2,10,80,8,128]{4,3,2,1,0:T(8,128)} %param.5), kind=kLoop, calls=%fused_computation.67 | loop fusion | bytes 22937600 | tf_op jit(solution)/shard_map/slice | solution.py:48
  26.6 0.0 slice-start
  26.6 7.6 %fusion.3 = (f32[2,10,80,2,3]{4,3,2,1,0:T(2,128)S(1)}, f32[2,10,80,2,3]{4,3,2,1,0:T(2,128)S(1)}) fusion(f32[2,10,80,8,128]{4,3,2,1,0:T(8,128)} %param.5), kind=kLoop, calls=%fused_computation.66 | loop fusion | bytes 153600 | tf_op jit(solution)/shard_map/slice | solution.py:89
  34.2 0.0 copy-start.7
  34.2 0.0 copy-start.6
  34.2 0.0 slice-start.1
  34.2 5.1 %slice.173 = f32[2,10,80,2,128]{4,3,2,1,0:T(2,128)} slice(f32[2,10,80,8,128]{4,3,2,1,0:T(8,128)} %param.5), slice={[0:2], [0:10], [0:80], [3:5], [0:128]} | slice | bytes 3276800 | tf_op jit(solution)/shard_map/slice | solution.py:85
  39.3 0.0 copy-done.7
  39.3 0.1 iota_compare_fusion
  39.4 0.0 copy-done.6
  39.4 0.1 select_reduce_fusion
  39.6 0.0 copy-start.1
  39.6 1.3 copy.26
  40.9 1.3 copy.25
  42.2 0.0 slice-done
  42.2 0.0 slice-done.1
  42.2 1.5 copy-done.1
  43.6 2.0 copy_subtract_fusion
  45.6 0.0 collective-permute-done
  45.7 1.1 constant_dynamic-update-slice_fusion.2
  46.7 0.0 copy-start.4
  46.7 0.0 copy-start.5
  46.7 1.8 constant_dynamic-update-slice_fusion.1
  48.6 0.1 copy-done.4
  48.6 0.5 copy-done.5
  49.1 1.3 pad_maximum_fusion
  50.5 0.9 slice_subtract_fusion
  51.4 0.0 collective-permute-done.1
  51.5 1.3 collective-permute-start.3
  52.8 4.7 %collective-permute-start.2 = (f32[2,16,3,2,128]{4,2,3,1,0:T(4,128)S(1)}, f32[2,16,3,2,128]{4,2,3,1,0:T(4,128)S(1)}, u32[]{:S(2)}, u32[]{:S(2)}) collective-permute-start(f32[2,16,3,2,128]{4,2,3,1,0:T(4,128)S(1)} %get-tuple-element.35), channel_id=1, source_target_pairs={{0,1},{2,3},{4,5},{6,7},{8,9},{10,11},{12,13},{14,15},{16,17},{18,... | collective-permute-start | bytes 294920 | tf_op jit(solution)/shard_map/ppermute | solution.py:18
  57.5 0.2 slice_subtract_fusion.1
  57.7 0.6 collective-permute-done.3
  58.4 1.6 collective-permute-done.2
  60.0 0.4 pad_maximum_fusion.1
  60.4 0.0 copy-start.2
  60.4 0.2 slice_subtract_fusion.2
  60.6 1.2 copy-done.2
  61.8 30.9 %multiply_subtract_fusion = f32[2,10,80,2,128]{4,2,3,1,0:T(8,128)} fusion(f32[2,10,80,7,128]{4,2,3,1,0:T(8,128)S(1)} %copy_subtract_fusion, f32[2,10,80,2,133]{4,2,3,1,0:T(8,128)S(1)} %slice_subtract_fusion, f32[2,10,85,2,128]{4,2,3,1,0:T(8,128)S(1)} %slice_subtract_fusion.2, f32[2,15,80,2,128]{4,2,3,1,0:T(8,128)S(1)} %slice_subtract_fusion.1, ...), kind=kLoop, calls=%fused_computation.14 | loop fusion | flops 216268800 | bytes 42599480 | tf_op jit(solution)/shard_map/sub | solution.py:79
  92.7 0.0 all-gather.2.cloned.1.call-update
  92.7 0.0 copy-done
  92.7 0.7 constant_dynamic-slice_fusion.1
  93.4 0.3 slice_reduce_fusion.7
  93.7 0.3 compare_reduce_fusion.7
  94.1 0.0 copy-start.3
  94.1 123.0 %all-gather.2.cloned.1.call-done = f32[8,10,80,2,128]{4,2,3,1,0:T(8,128)} async-done(((f32[2,10,80,2,128]{4,2,3,1,0:T(8,128)}), f32[8,10,80,2,128]{4,2,3,1,0:T(8,128)}) %all-gather.2.cloned.1.call-update) | async-done | bytes 6553616 | tf_op jit(solution)/shard_map/all_gather | solution.py:112
  217.1 3.3 %slice_bitcast_fusion.7 = (f32[10,80,2,128]{3,1,2,0:T(8,128)S(1)}, f32[10,80,2,128]{3,1,2,0:T(8,128)S(1)}, f32[10,80,2,128]{3,1,2,0:T(8,128)S(1)}, f32[10,80,2,1...) fusion(f32[8,10,80,2,128]{4,2,3,1,0:T(8,128)} %all-gather.2.clo, ...), kind=kLoop, calls=%fused_computation.22 | loop fusion | bytes 13107200 | tf_op jit(solution)/shard_map/add | solution.py:120
  220.4 0.0 copy-done.3
  220.5 1.4 minimum_select_fusion
  221.9 2.0 copy.21
  (12 shorter events, 0.2 us)
Async XLA Ops:
  6.5 86.2 %copy-start = (f32[8,8]{1,0:T(8,128)S(1)}, f32[8,8]{1,0:T(8,128)}, u32[]{:S(2)}) copy-start(f32[8,8]{1,0:T(8,128)} %param.9) | copy-start | bytes 772
  6.5 210.6 %all-gather.2.cloned.1.call-start = ((), (), s32[]{:S(2)}) async-start(), calls=%async_computation | async-start | bytes 8192000 | tf_op jit(solution)/shard_map/all_gather | solution.py:112
  10.0 35.6 %collective-permute-start = (f32[2,3,80,2,128]{4,2,3,1,0:T(8,128)}, f32[2,3,80,2,128]{4,2,3,1,0:T(8,128)}, u32[]{:S(2)}, u32[]{:S(2)}) collective-permute-start(f32[2,3,80,2,128]{4,2,3,1,0:T(8,128)} %copy.23), channel_id=1, source_target_pairs={{0,2},{2,4},{4,6},{1,3},{3,5},{5,7},{8,10},{10,12},{12,14},{9,11},... | collective-permute-start | bytes 1474568 | tf_op jit(solution)/shard_map/ppermute | solution.py:18
  14.0 37.4 %collective-permute-start.1 = (f32[2,3,80,2,128]{4,2,3,1,0:T(8,128)}, f32[2,3,80,2,128]{4,2,3,1,0:T(8,128)S(1)}, u32[]{:S(2)}, u32[]{:S(2)}) collective-permute-start(f32[2,3,80,2,128]{4,2,3,1,0:T(8,128)} %copy.24), channel_id=1, source_target_pairs={{2,0},{4,2},{6,4},{3,1},{5,3},{7,5},{10,8},{12,10},{14,12},{11,9},... | collective-permute-start | bytes 1474568 | tf_op jit(solution)/shard_map/ppermute | solution.py:20
  26.6 15.6 %slice-start = ((s8[6553600]{0:T(1024)(128)(4,1)}), s8[4194304]{0:T(1024)(128)(4,1)S(1)}, s32[]{:S(2)}) async-start(s8[6553600]{0:T(1024)(128)(4,1)} %bitcast.26), calls=%async_computation.1 | async-start | bytes 8388608
  34.2 5.1 %copy-start.7 = (s32[2]{0:T(128)S(1)}, s32[2]{0:T(128)}, u32[]{:S(2)}) copy-start(s32[2]{0:T(128)} %param.7) | copy-start | bytes 28
  34.2 5.2 %copy-start.6 = (f32[3,4]{1,0:T(4,128)S(1)}, f32[3,4]{1,0:T(4,128)}, u32[]{:S(2)}) copy-start(f32[3,4]{1,0:T(4,128)} %param.6) | copy-start | bytes 148
  34.2 7.9 %slice-start.1 = ((s8[6553600]{0:T(1024)(128)(4,1)}), s8[2359296]{0:T(1024)(128)(4,1)S(1)}, s32[]{:S(2)}) async-start(s8[6553600]{0:T(1024)(128)(4,1)} %bitcast.26), calls=%async_computation.2 | async-start | bytes 4718592
  39.6 4.0 %copy-start.1 = (f32[2,10,80,7,128]{4,3,2,1,0:T(8,128)S(1)}, f32[2,10,80,7,128]{4,3,2,1,0:T(8,128)}, u32[]{:S(2)}) copy-start(f32[2,10,80,7,128]{4,3,2,1,0:T(8,128)} %get-tuple-element.34) | copy-start | bytes 17203204
  46.7 1.9 copy-start.4
  46.7 2.4 %copy-start.5 = (f32[2,10,80,2,3]{4,2,3,1,0:T(8,128)S(1)}, f32[2,10,80,2,3]{4,2,3,1,0:T(8,128)}, u32[]{:S(2)}) copy-start(f32[2,10,80,2,3]{4,2,3,1,0:T(8,128)} %copy.25) | copy-start | bytes 115204
  51.5 6.9 %collective-permute-start.3 = (f32[2,16,3,2,128]{4,2,3,1,0:T(4,128)S(1)}, f32[2,16,3,2,128]{4,2,3,1,0:T(4,128)S(1)}, u32[]{:S(2)}, u32[]{:S(2)}) collective-permute-start(f32[2,16,3,2,128]{4,2,3,1,0:T(4,128)S(1)} %get-tuple-element.36), channel_id=1, source_target_pairs={{1,0},{3,2},{5,4},{7,6},{9,8},{11,10},{13,12},{15,14},{17,16},{19,... | collective-permute-start | bytes 294920 | tf_op jit(solution)/shard_map/ppermute | solution.py:20
  52.8 7.2 %collective-permute-start.2 = (f32[2,16,3,2,128]{4,2,3,1,0:T(4,128)S(1)}, f32[2,16,3,2,128]{4,2,3,1,0:T(4,128)S(1)}, u32[]{:S(2)}, u32[]{:S(2)}) collective-permute-start(f32[2,16,3,2,128]{4,2,3,1,0:T(4,128)S(1)} %get-tuple-element.35), channel_id=1, source_target_pairs={{0,1},{2,3},{4,5},{6,7},{8,9},{10,11},{12,13},{14,15},{16,17},{18,... | collective-permute-start | bytes 294920 | tf_op jit(solution)/shard_map/ppermute | solution.py:18
  60.4 1.4 copy-start.2
  94.1 126.4 %copy-start.3 = (f32[2,10,80,2,128]{4,2,3,1,0:T(8,128)S(1)}, f32[2,10,80,2,128]{4,2,3,1,0:T(8,128)}, u32[]{:S(2)}) copy-start(f32[2,10,80,2,128]{4,2,3,1,0:T(8,128)} %multiply_subtract_fusion) | copy-start | bytes 4915204
Sparse Core Ops, SparseCore 0:
  92.8 124.2 all-gather.1
where the time goes:
time: 231 us
  waiting for transfers between devices  125 us (54%)
  local copies, waits for them, and re-layouts  43.5 us (19%)
  other arithmetic  37.8 us (16%)
  between operations  13.7 us (6%)
  starting transfers between devices  10.4 us (5%)
    all_gather x1, waiting for transfers between devices, shards(): shard_piece = lax.all_gather(updated, 'mode', axis=0, tiled=True)  123 us
    sub x1, other arithmetic, section_update(): return centre - time_step * (hamiltonian - 0.5 * dissipation)  30.9 us
    slice x1, local copies, waits for them, and re-layouts, weno_pair(): lax.slice_in_dim(extended, 1, length + 6, axis=axis_no)  11.3 us
    unnamed x26, local copies, waits for them, and re-layouts  10.4 us
    ppermute x2, starting transfers between devices, extended_2(): lax.ppermute(tail, axis, [(i, (i + 1) % count) for i in range(ends)])  7.87 us
    slice x1, local copies, waits for them, and re-layouts, shards(): centre[..., -3:]  7.62 us
    slice x1, local copies, waits for them, and re-layouts, shards(): centre = values[:, :, :, 3:3 + planes]  5.11 us
  transfers between devices with their start and end apart: 5, of which 3 were waited for; matrix products, arithmetic and copies ran while one was open for 16% of the time, Pallas kernels for 0%

commit v1 on v0

v1 whole, which is shorter than its diff:
```python
import functools

import jax
import jax.numpy as jnp
from jax import lax
from jax.experimental import pallas as pl
from jax.experimental.pallas import tpu as pltpu
from jax.sharding import PartitionSpec as P

epsilon = 1e-06
time_step = 0.1
MESH = pl.DeviceIdType.MESH
REACH = 3
PAD = 8
TILE = 8
BLOCK = 16
OUT_LAG = 4


def line_place(n):
    z = lax.axis_index("mode")
    half = n // 2
    left = z < half
    h = jnp.where(left, z, n - 1 - z)
    return z, left, h


def plan_kernel(n, per, reduce, mask, cost, table, kinds, coef, send, take, rank):
    z, left, h = line_place(n)
    half = n // 2
    side = per * half
    big = jnp.float32(jnp.inf)

    def mode_of(on_left, i):
        dev = i // per
        return per * jnp.where(on_left, dev, n - 1 - dev) + i % per

    def edge(target, source):
        ok = (mask[target, source] == 1) & (target != source)
        return jnp.where(ok, cost[target, source], big)

    for m in range(per):
        kind = kinds[m]
        for j in range(3):
            coef[m, j] = table[j, kind]

    def cover(from_left):
        rows = []
        for t in range(side):
            bits = jnp.int32(0)
            for i in range(side):
                hit = mask[mode_of(~from_left, t), mode_of(from_left, i)] == 1
                bits = bits + jnp.where(hit, jnp.int32(1 << i), jnp.int32(0))
            rows.append(bits)

        def size_of(chosen):
            total = jnp.int32(0)
            for i in range(side):
                total = total + ((chosen >> i) & 1)
            for t in range(side):
                total = total + jnp.where((rows[t] & ~chosen) != 0, 1, 0)
            return total

        everything = jnp.int32((1 << side) - 1)
        if not reduce:
            return rows, everything, jnp.int32(side)

        def better(s, best):
            size = size_of(s)
            win = size < best[1]
            return jnp.where(win, s, best[0]), jnp.where(win, size, best[1])

        chosen, size = lax.fori_loop(
            0, (1 << side) - 1, better, (everything, jnp.int32(side))
        )
        return rows, chosen, size

    for j in range(side):
        for i in range(side):
            send[j, i] = big
    for row in range(per + side):
        for col in range(per + 2 * side):
            take[row, col] = big

    own = [mode_of(left, per * h + m) for m in range(per)]
    for m in range(per):
        for o in range(per):
            take[m, o] = edge(own[m], own[o])
        for i in range(side - per):
            take[m, per + i] = edge(own[m], mode_of(left, i))
    for j in range(side - per):
        for o in range(per):
            take[per + j, o] = edge(mode_of(left, j), own[o])

    rows_out, set_out, size_out = cover(left)
    rows_in, set_in, size_in = cover(~left)
    rank[0] = jnp.maximum(size_out, size_in)

    @pl.when(h < half - 1)
    def _():
        for j in range(side):
            for m in range(per):
                take[m, per + side + j] = jnp.where(j == per * h + m, 0.0, big)
            if j < side - per:
                take[per + j, per + side + j] = 0.0

    @pl.when(h == half - 1)
    def _():
        place = jnp.int32(0)
        for i in range(side):
            inside = ((set_out >> i) & 1) == 1
            at = place

            @pl.when(inside)
            def _():
                send[at, i] = 0.0

            place = place + jnp.where(inside, 1, 0)
        for t in range(side):
            inside = (rows_out[t] & ~set_out) != 0
            at = place

            @pl.when(inside)
            def _():
                for i in range(side):
                    send[at, i] = edge(mode_of(~left, t), mode_of(left, i))

            place = place + jnp.where(inside, 1, 0)
        row_of = [per + t if t < side - per else t - (side - per) for t in range(side)]
        place = jnp.int32(0)
        for i in range(side):
            inside = ((set_in >> i) & 1) == 1
            at = place

            @pl.when(inside)
            def _():
                for t in range(side):
                    take[row_of[t], per + side + at] = edge(mode_of(left, t), mode_of(~left, i))

            place = place + jnp.where(inside, 1, 0)
        for t in range(side):
            inside = (rows_in[t] & ~set_in) != 0
            at = place

            @pl.when(inside)
            def _():
                take[row_of[t], per + side + at] = 0.0

            place = place + jnp.where(inside, 1, 0)


def weno_cells(u, count):
    d = [u[k + 1] - u[k] for k in range(count + 5)]
    e = [d[k + 1] - d[k] for k in range(count + 4)]
    e3 = [3.0 * e[k] for k in range(count + 4)]
    fs = [e[k + 1] - e[k] for k in range(count + 3)]
    g = [(13.0 / 3.0) * (f * f) + 4.0 * epsilon for f in fs]

    def squared(x, k):
        s = g[k] + x * x
        return s * s

    first = {k: squared(e[k] - e3[k + 1], k) for k in range(0, count + 1)}
    second = {k: squared(e[k] + e[k + 1], k) for k in range(1, count + 2)}
    third = {k: squared(e3[k] - e[k + 1], k) for k in range(2, count + 3)}

    def mix(a, b, c, x, y, w):
        wa = b * c
        wb = 6.0 * (a * c)
        wc = 3.0 * (a * b)
        return (wa * x + wb * y + wc * w) * pl.reciprocal(6.0 * (wa + wb + wc), approx=True)

    out = []
    for i in range(count):
        minus = d[i + 2] + mix(
            first[i],
            second[i + 1],
            third[i + 2],
            5.0 * e[i + 1] - 2.0 * e[i],
            e[i + 1] + 2.0 * e[i + 2],
            4.0 * e[i + 2] - e[i + 3],
        )
        plus = d[i + 3] - mix(
            third[i + 3],
            second[i + 2],
            first[i + 1],
            5.0 * e[i + 3] - 2.0 * e[i + 4],
            e[i + 3] + 2.0 * e[i + 2],
            4.0 * e[i + 2] - e[i + 1],
        )
        out.append((minus, plus))
    return out


def section_kernel(
    n, gx_count, gy_count, slots,
    coef, send_tab, take_tab, vals_hbm, out,
    vals, cells, fresh, outer_rx, inner_rx, in_slot, out_slot,
    load_sem, halo_send, halo_recv, in_send, in_recv, out_send, out_recv,
):
    per, rows, deep, lanes = vals.shape
    planes = cells.shape[0]
    cols = fresh.shape[3]
    depth = deep // cols
    tiles = cols // TILE
    half = n // 2
    side = per * half
    z, left, h = line_place(n)
    gx, gy = lax.axis_index("gx"), lax.axis_index("gy")
    inner_z = jnp.where(left, z + 1, z - 1)
    outer_z = jnp.where(left, z - 1, z + 1)

    loads = [
        pltpu.make_async_copy(vals_hbm.at[m], vals.at[m], load_sem.at[m]) for m in range(per)
    ]
    for copy in loads:
        copy.start()

    has = [gx > 0, gx < gx_count - 1, gy > 0, gy < gy_count - 1]
    barrier = pltpu.get_barrier_semaphore()
    peers = [
        (has[0], {"gx": gx - 1}),
        (has[1], {"gx": gx + 1}),
        (has[2], {"gy": gy - 1}),
        (has[3], {"gy": gy + 1}),
        (h > 0, {"mode": outer_z}),
        (h >= 0, {"mode": inner_z}),
    ]
    for there, who in peers:
        @pl.when(there)
        def _():
            pl.semaphore_signal(barrier, inc=1, device_id=who, device_id_type=MESH)

    for k, (there, lo) in enumerate([(has[0], 0), (has[1], REACH + rows)]):
        @pl.when(~there)
        def _():
            cells[:, :, lo : lo + REACH] = jnp.zeros(
                (planes, per, REACH) + cells.shape[3:], jnp.float32
            )
    for k, (there, lo) in enumerate([(has[2], 0), (has[3], PAD + cols)]):
        @pl.when(~there)
        def _():
            cells[:, :, REACH : REACH + rows, lo : lo + PAD] = jnp.zeros(
                (planes, per, rows, PAD, lanes), jnp.float32
            )

    for m in range(per):
        loads[m].wait()

        def pack(i, carry, m=m):
            for p in range(planes):
                cells[p, m, REACH + i, PAD : PAD + cols] = vals[
                    m, i, pl.ds(REACH + p, cols, stride=depth)
                ]
            return carry

        lax.fori_loop(0, rows, pack, 0)

    met = sum(there.astype(jnp.int32) for there, _ in peers)
    pl.semaphore_wait(barrier, met)

    inside = slice(PAD, PAD + cols)
    body_rows = slice(REACH, REACH + rows)

    def cut(r, c):
        return cells.at[:, :, r.start : r.stop, c.start : c.stop]

    spans = [
        (cut(slice(REACH, 2 * REACH), inside), cut(slice(REACH + rows, 2 * REACH + rows), inside)),
        (cut(slice(rows, REACH + rows), inside), cut(slice(0, REACH), inside)),
        (cut(body_rows, slice(PAD, 2 * PAD)), cut(body_rows, slice(PAD + cols, 2 * PAD + cols))),
        (cut(body_rows, slice(cols, PAD + cols)), cut(body_rows, slice(0, PAD))),
    ]
    halos = [
        pltpu.make_async_remote_copy(
            src_ref=src,
            dst_ref=dst,
            send_sem=halo_send.at[k],
            recv_sem=halo_recv.at[k],
            device_id=peers[k][1],
            device_id_type=MESH,
        )
        for k, (src, dst) in enumerate(spans)
    ]
    for k in (2, 3, 1, 0):
        @pl.when(has[k])
        def _():
            halos[k].start()

    for k, there in ((3, has[2]), (2, has[3])):
        @pl.when(there)
        def _():
            halos[k].wait_recv()

    lane = lax.broadcasted_iota(jnp.int32, (TILE, lanes), 1).astype(jnp.float32)
    heading = 2.0 * jnp.pi * lane / lanes
    cosine, sine = jnp.cos(heading), jnp.sin(heading)
    top = 1.0 + 0.5 * (planes - 1)

    def row_at(s):
        return lax.rem(s + REACH, rows)

    def update_row(row):
        for m in range(per):
            shift, raw, accel = coef[m, 0], coef[m, 1], coef[m, 2]
            turn = 0.5 + jnp.abs(raw)
            side_one = 0.5 * (top + jnp.abs(shift))
            side_four = 0.5 * jnp.abs(accel)

            def tile(t, carry):
                base = pl.multiple_of(t * TILE, TILE)
                stack = [
                    vals[m, row, pl.ds(base * depth + j, TILE, stride=depth)]
                    for j in range(planes + 2 * REACH)
                ]
                four = weno_cells(stack, planes)
                for p in range(planes):
                    speed = 1.0 + 0.5 * p
                    centre = stack[REACH + p]
                    lane_shift = [
                        centre if k == REACH else pltpu.roll(centre, (REACH - k) % lanes, 1)
                        for k in range(2 * REACH + 1)
                    ]
                    one = weno_cells(
                        [
                            cells[p, m, row + k, pl.ds(base + PAD, TILE)]
                            for k in range(2 * REACH + 1)
                        ],
                        1,
                    )[0]
                    two = weno_cells(
                        [
                            cells[p, m, row + REACH, pl.ds(base + (PAD - REACH + k), TILE)]
                            for k in range(2 * REACH + 1)
                        ],
                        1,
                    )[0]
                    three = weno_cells(lane_shift, 1)[0]
                    total = (0.5 * (speed * cosine - shift)) * (one[0] + one[1])
                    total = total - side_one * (one[1] - one[0])
                    total = total + (0.5 * speed * sine) * (two[0] + two[1])
                    total = total - (0.5 * top) * (two[1] - two[0])
                    total = total + (0.5 * turn) * (
                        jnp.abs(three[0] + three[1]) - (three[1] - three[0])
                    )
                    total = total + (0.5 * accel) * (four[p][0] + four[p][1])
                    total = total - side_four * (four[p][1] - four[p][0])
                    fresh[row, m, p, pl.ds(base, TILE)] = centre - time_step * total
                return carry

            lax.fori_loop(0, tiles, tile, 0)

    def inward_copies(hh, row):
        if hh == half - 1:
            return [
                pltpu.make_async_remote_copy(
                    src_ref=in_slot.at[row],
                    dst_ref=inner_rx.at[row, pl.ds(0, slots)],
                    send_sem=in_send.at[row, 0],
                    recv_sem=out_recv.at[row],
                    device_id={"mode": inner_z},
                    device_id_type=MESH,
                )
            ]
        copies = [
            pltpu.make_async_remote_copy(
                src_ref=fresh.at[row],
                dst_ref=outer_rx.at[row, pl.ds(per * hh, per)],
                send_sem=in_send.at[row, 0],
                recv_sem=in_recv.at[row, 0],
                device_id={"mode": inner_z},
                device_id_type=MESH,
            )
        ]
        if hh > 0:
            copies.append(
                pltpu.make_async_remote_copy(
                    src_ref=outer_rx.at[row, pl.ds(0, per * hh)],
                    dst_ref=outer_rx.at[row, pl.ds(0, per * hh)],
                    send_sem=in_send.at[row, 1],
                    recv_sem=in_recv.at[row, 1],
                    device_id={"mode": inner_z},
                    device_id_type=MESH,
                )
            )
        return copies

    def outward_copy(hh, row):
        return pltpu.make_async_remote_copy(
            src_ref=out_slot.at[row, pl.ds(0, per * hh)],
            dst_ref=inner_rx.at[row, pl.ds(0, per * hh)],
            send_sem=out_send.at[row],
            recv_sem=out_recv.at[row],
            device_id={"mode": outer_z},
            device_id_type=MESH,
        )

    def least(start, pairs):
        best = start
        for value, weight in pairs:
            best = value + weight if best is None else jnp.minimum(best, value + weight)
        return best

    def each_stage(body):
        for hh in range(half):
            @pl.when(h == hh)
            def _():
                body(hh)

    blocks = cols // BLOCK

    def inward(row):
        def stage(hh):
            if hh > 0:
                for copy in inward_copies(hh - 1, row):
                    copy.wait_recv()
            if hh == half - 1:
                def block(b, carry):
                    span = pl.ds(pl.multiple_of(b * BLOCK, BLOCK), BLOCK)
                    for p in range(planes):
                        given = [outer_rx[row, i, p, span] for i in range(per * hh)]
                        given += [fresh[row, m, p, span] for m in range(per)]
                        for j in range(slots):
                            in_slot[row, j, p, span] = least(
                                None, [(given[i], send_tab[j, i]) for i in range(side)]
                            )
                    return carry

                lax.fori_loop(0, blocks, block, 0)
            for copy in inward_copies(hh, row):
                copy.start()

        each_stage(stage)

    def outward(row):
        def stage(hh):
            mid = hh == half - 1
            arrived = slots if mid else per * (hh + 1)
            if mid:
                inward_copies(hh, row)[0].wait_recv()
            else:
                outward_copy(hh + 1, row).wait_recv()

            def block(b, carry):
                start = pl.multiple_of(b * BLOCK, BLOCK)
                span = pl.ds(start, BLOCK)
                for p in range(planes):
                    own = [fresh[row, m, p, span] for m in range(per)]
                    outer = [outer_rx[row, i, p, span] for i in range(per * hh)]
                    inner = [inner_rx[row, j, p, span] for j in range(arrived)]
                    base = per + side
                    for j in range(per * hh):
                        pairs = [(own[m], take_tab[per + j, m]) for m in range(per)]
                        if mid:
                            pairs += [
                                (inner[k], take_tab[per + j, base + k]) for k in range(arrived)
                            ]
                            out_slot[row, j, p, span] = least(None, pairs)
                        else:
                            out_slot[row, j, p, span] = least(inner[j], pairs)
                    for m in range(per):
                        pairs = [(own[o], take_tab[m, o]) for o in range(per) if o != m]
                        pairs += [(outer[i], take_tab[m, per + i]) for i in range(per * hh)]
                        if mid:
                            pairs += [(inner[k], take_tab[m, base + k]) for k in range(arrived)]
                            best = least(own[m], pairs)
                        else:
                            best = least(jnp.minimum(own[m], inner[per * hh + m]), pairs)
                        out[m, row, pl.ds(start * planes + p, BLOCK, stride=planes)] = best
                return carry

            lax.fori_loop(0, blocks, block, 0)
            if hh > 0:
                outward_copy(hh, row).start()

        each_stage(stage)

    def step(s, carry):
        @pl.when((s == rows - 2 * REACH) & has[1])
        def _():
            halos[0].wait_recv()

        @pl.when((s == rows - REACH) & has[0])
        def _():
            halos[1].wait_recv()

        update_row(row_at(s))
        inward(row_at(s))

        @pl.when(s >= OUT_LAG)
        def _():
            outward(row_at(s - OUT_LAG))

        return carry

    lax.fori_loop(0, rows, step, 0)

    def rest(s, carry):
        outward(row_at(s))
        return carry

    lax.fori_loop(rows - OUT_LAG, rows, rest, 0)

    for k in range(4):
        @pl.when(has[k])
        def _():
            halos[k].wait_send()

    def finish(row, carry):
        def stage(hh):
            for copy in inward_copies(hh, row):
                copy.wait_send()
            if hh > 0:
                outward_copy(hh, row).wait_send()

        each_stage(stage)
        return carry

    lax.fori_loop(0, rows, finish, 0)


def smem():
    return pl.BlockSpec(memory_space=pltpu.SMEM)


def shards(n, gx_count, gy_count, values, coef_table, mode_coef, switch_mask, switch_cost):
    per, rows, cols, depth, lanes = values.shape
    planes = depth - 2 * REACH
    side = per * (n // 2)
    f32 = jnp.float32
    coef, send_tab, take_tab, rank = pl.pallas_call(
        functools.partial(plan_kernel, n, per, False),
        out_shape=(
            jax.ShapeDtypeStruct((per, 3), f32),
            jax.ShapeDtypeStruct((side, side), f32),
            jax.ShapeDtypeStruct((per + side, per + 2 * side), f32),
            jax.ShapeDtypeStruct((1,), jnp.int32),
        ),
        in_specs=[smem()] * 4,
        out_specs=(smem(),) * 4,
        name="plan",
    )(switch_mask, switch_cost, coef_table, mode_coef)
    slots = side
    piece = (planes, cols, lanes)
    dma = pltpu.SemaphoreType.DMA
    out = pl.pallas_call(
        functools.partial(section_kernel, n, gx_count, gy_count, slots),
        out_shape=jax.ShapeDtypeStruct((per, rows, cols * planes, lanes), f32),
        in_specs=[smem()] * 3 + [pl.BlockSpec(memory_space=pl.ANY)],
        out_specs=pl.BlockSpec(memory_space=pltpu.VMEM),
        scratch_shapes=[
            pltpu.VMEM((per, rows, cols * depth, lanes), f32),
            pltpu.VMEM((planes, per, rows + 2 * REACH, cols + 2 * PAD, lanes), f32),
            pltpu.VMEM((rows, per) + piece, f32),
            pltpu.VMEM((rows, max(side - per, 1)) + piece, f32),
            pltpu.VMEM((rows, side) + piece, f32),
            pltpu.VMEM((rows, slots) + piece, f32),
            pltpu.VMEM((rows, max(side - per, 1)) + piece, f32),
            dma((per,)),
            dma((4,)),
            dma((4,)),
            dma((rows, 2)),
            dma((rows, 2)),
            dma((rows,)),
            dma((rows,)),
        ],
        compiler_params=pltpu.CompilerParams(
            collective_id=0, has_side_effects=True, vmem_limit_bytes=58 * 1024 * 1024
        ),
        name="section",
    )(coef, send_tab, take_tab, values.reshape(per, rows, cols * depth, lanes))
    return out.reshape(per, rows, cols, planes, lanes)


def solution(mesh):
    in_specs = (P("mode", "gx", "gy", None, None), P(), P("mode"), P(), P())
    out_specs = P("mode", "gx", "gy", None, None)
    body = functools.partial(shards, mesh.shape["mode"], mesh.shape["gx"], mesh.shape["gy"])
    return jax.shard_map(body, mesh=mesh, in_specs=in_specs, out_specs=out_specs, check_vma=False)
```

time: 231 us -> 111 us (0.48)
  waiting for transfers between devices: 125 us -> 0 us
  Pallas kernels: 0 us -> 108 us
  local copies, waits for them, and re-layouts: 43.5 us -> 2.71 us
  other arithmetic: 37.8 us -> 0 us
  between operations: 13.7 us -> 0.02 us
  starting transfers between devices: 10.4 us -> 0 us
    all_gather x1 -> x0, waiting for transfers between devices: 123 us -> none  [shards(): shard_piece = lax.all_gather(updated, 'mode', axis=0, tiled=True)]
    pallas_call x0 -> x2, Pallas kernels: none -> 108 us  [the longest x1 106 us: shards(): pl.pallas_call(functools.partial(section_kernel, n, gx_count, gy_count, s...]
    sub x6 -> x0, other arithmetic: 34.1 us -> none  [the longest x1 30.9 us: section_update(): return centre - time_step * (hamiltonian - 0.5 * dissipation)]
    slice x5 -> x0, local copies, waits for them, and re-layouts: 26.7 us -> none  [the longest x1 11.3 us: weno_pair(): lax.slice_in_dim(extended, 1, length + 6, axis=axis_no)]
    ppermute x4 -> x0, starting transfers between devices: 10.4 us -> none  [the longest x2 7.87 us: extended_2(): lax.ppermute(tail, axis, [(i, (i + 1) % count) for i in range(ends)])]
    unnamed x26 -> x1, local copies, waits for them, and re-layouts: 10.4 us -> 2.71 us
    add x1 -> x0, local copies, waits for them, and re-layouts: 3.3 us -> none  [shards(): candidate = shard_piece[k][None] + cost_here.reshape(column_shape)]
  transfers between devices with their start and end apart: 5 -> 0, of which waited for: 3 -> 0; matrix products, arithmetic and copies ran while one was open for 16% -> 0% of each run, Pallas kernels for 0% -> 0%
where the time goes in v1:
time: 111 us
  Pallas kernels  108 us (97%)
  local copies, waits for them, and re-layouts  2.71 us (2%)
    pallas_call x1, Pallas kernels, shards(): pl.pallas_call(functools.partial(section_kernel, n, gx_count, gy_count, s...  106 us
    unnamed x1, local copies, waits for them, and re-layouts  2.71 us

profile of v1, /device:TPU:0, one launch (start us, length us, event | category | flops | bytes accessed | tf_op | source)
XLA Modules:
  0.0 110.5 jit_solution(17852070065037576674)
XLA Ops:
  0.0 1.7 %plan.1 = (f32[2,3]{1,0:T(2,128)}, f32[4,4]{1,0:T(4,128)}, f32[6,10]{1,0:T(8,128)}, s32[1]{0:T(128)}) custom-call(s32[8,8]{1,0:T(8,128)} %mask.1, f32[8,8]{1,0:T(8,128)} %cost.1, f32[3,4]{1,0:T(4,128)} %table.1, s32[2]{0:T(128)} %kinds.1), custom_call_target="tpu_custom_call" | custom-call | tf_op jit(solution)/shard_map/plan/pallas_call | solution.py:531
  1.7 106.1 %section.1 = f32[2,10,160,128]{3,2,1,0:T(8,128)} custom-call(f32[2,3]{1,0:T(2,128)} %get-tuple-element.8.coef, f32[4,4]{1,0:T(4,128)} %get-tuple-element.9.send_tab, f32[6,10]{1,0:T(8,128)} %get-tuple-element.10.take_tab, f32[2,10,640,128]{3,2,1,0:T(8,128)} %bitcast.2), custom_call_target="tpu_custom_call" | custom-call | tf_op jit(solution)/shard_map/section/pallas_call | solution.py:546
  107.8 2.7 %copy.7 = f32[2,10,80,2,128]{4,3,2,1,0:T(2,128)} copy(f32[2,10,80,2,128]{4,3,2,1,0:T(2,128)} %bitcast.3) | data formatting | bytes 3276800

commit v2 on v1

--- a/solution.py
+++ b/solution.py
@@ -14,7 +14,7 @@
 PAD = 8
 TILE = 8
 BLOCK = 16
-OUT_LAG = 4
+OUT_LAG = 3
 
 
 def line_place(n):
@@ -25,7 +25,7 @@
     return z, left, h
 
 
-def plan_kernel(n, per, reduce, mask, cost, table, kinds, coef, send, take, rank):
+def plan_kernel(n, per, mask, cost, table, kinds, coef, send, take, rank):
     z, left, h = line_place(n)
     half = n // 2
     side = per * half
@@ -62,8 +62,6 @@
             return total
 
         everything = jnp.int32((1 << side) - 1)
-        if not reduce:
-            return rows, everything, jnp.int32(side)
 
         def better(s, best):
             size = size_of(s)
@@ -409,71 +407,71 @@
 
     blocks = cols // BLOCK
 
-    def inward(row):
-        def stage(hh):
-            if hh > 0:
-                for copy in inward_copies(hh - 1, row):
-                    copy.wait_recv()
-            if hh == half - 1:
-                def block(b, carry):
-                    span = pl.ds(pl.multiple_of(b * BLOCK, BLOCK), BLOCK)
-                    for p in range(planes):
-                        given = [outer_rx[row, i, p, span] for i in range(per * hh)]
-                        given += [fresh[row, m, p, span] for m in range(per)]
-                        for j in range(slots):
-                            in_slot[row, j, p, span] = least(
-                                None, [(given[i], send_tab[j, i]) for i in range(side)]
-                            )
-                    return carry
-
-                lax.fori_loop(0, blocks, block, 0)
-            for copy in inward_copies(hh, row):
-                copy.start()
-
-        each_stage(stage)
-
-    def outward(row):
-        def stage(hh):
-            mid = hh == half - 1
-            arrived = slots if mid else per * (hh + 1)
-            if mid:
-                inward_copies(hh, row)[0].wait_recv()
-            else:
-                outward_copy(hh + 1, row).wait_recv()
-
+    def inward(hh, row):
+        if hh > 0:
+            for copy in inward_copies(hh - 1, row):
+                copy.wait_recv()
+        if hh == half - 1:
             def block(b, carry):
-                start = pl.multiple_of(b * BLOCK, BLOCK)
-                span = pl.ds(start, BLOCK)
+                span = pl.ds(pl.multiple_of(b * BLOCK, BLOCK), BLOCK)
                 for p in range(planes):
-                    own = [fresh[row, m, p, span] for m in range(per)]
-                    outer = [outer_rx[row, i, p, span] for i in range(per * hh)]
-                    inner = [inner_rx[row, j, p, span] for j in range(arrived)]
-                    base = per + side
-                    for j in range(per * hh):
-                        pairs = [(own[m], take_tab[per + j, m]) for m in range(per)]
-                        if mid:
-                            pairs += [
-                                (inner[k], take_tab[per + j, base + k]) for k in range(arrived)
-                            ]
-                            out_slot[row, j, p, span] = least(None, pairs)
-                        else:
-                            out_slot[row, j, p, span] = least(inner[j], pairs)
-                    for m in range(per):
-                        pairs = [(own[o], take_tab[m, o]) for o in range(per) if o != m]
-                        pairs += [(outer[i], take_tab[m, per + i]) for i in range(per * hh)]
-                        if mid:
-                            pairs += [(inner[k], take_tab[m, base + k]) for k in range(arrived)]
-                            best = least(own[m], pairs)
-                        else:
-                            best = least(jnp.minimum(own[m], inner[per * hh + m]), pairs)
-                        out[m, row, pl.ds(start * planes + p, BLOCK, stride=planes)] = best
+                    given = [outer_rx[row, i, p, span] for i in range(per * hh)]
+                    given += [fresh[row, m, p, span] for m in range(per)]
+                    for j in range(slots):
+                        in_slot[row, j, p, span] = least(
+                            None, [(given[i], send_tab[j, i]) for i in range(side)]
+                        )
                 return carry
 
             lax.fori_loop(0, blocks, block, 0)
-            if hh > 0:
-                outward_copy(hh, row).start()
-
-        each_stage(stage)
+        for copy in inward_copies(hh, row):
+            copy.start()
+
+    def outward(hh, row):
+        mid = hh == half - 1
+        arrived = slots if mid else per * (hh + 1)
+        if mid:
+            inward_copies(hh, row)[0].wait_recv()
+        else:
+            outward_copy(hh + 1, row).wait_recv()
+
+        def block(b, carry):
+            start = pl.multiple_of(b * BLOCK, BLOCK)
+            span = pl.ds(start, BLOCK)
+            for p in range(planes):
+                own = [fresh[row, m, p, span] for m in range(per)]
+                outer = [outer_rx[row, i, p, span] for i in range(per * hh)]
+                inner = [inner_rx[row, j, p, span] for j in range(arrived)]
+                base = per + side
+                for j in range(per * hh):
+                    pairs = [(own[m], take_tab[per + j, m]) for m in range(per)]
+                    if mid:
+                        pairs += [
+                            (inner[k], take_tab[per + j, base + k]) for k in range(arrived)
+                        ]
+                        out_slot[row, j, p, span] = least(None, pairs)
+                    else:
+                        out_slot[row, j, p, span] = least(inner[j], pairs)
+                for m in range(per):
+                    pairs = [(own[o], take_tab[m, o]) for o in range(per) if o != m]
+                    pairs += [(outer[i], take_tab[m, per + i]) for i in range(per * hh)]
+                    if mid:
+                        pairs += [(inner[k], take_tab[m, base + k]) for k in range(arrived)]
+                        best = least(own[m], pairs)
+                    else:
+                        best = least(jnp.minimum(own[m], inner[per * hh + m]), pairs)
+                    out[m, row, pl.ds(start * planes + p, BLOCK, stride=planes)] = best
+            return carry
+
+        lax.fori_loop(0, blocks, block, 0)
+        if hh > 0:
+            outward_copy(hh, row).start()
+
+    in_lag = [hh for hh in range(half)]
+    out_lag = [
+        rows if hh == 0 and half > 1 else hh + OUT_LAG + 2 * (half - 1 - hh)
+        for hh in range(half)
+    ]
 
     def step(s, carry):
         @pl.when((s == rows - 2 * REACH) & has[1])
@@ -484,22 +482,23 @@
         def _():
             halos[1].wait_recv()
 
-        update_row(row_at(s))
-        inward(row_at(s))
-
-        @pl.when(s >= OUT_LAG)
-        def _():
-            outward(row_at(s - OUT_LAG))
-
+        @pl.when(s < rows)
+        def _():
+            update_row(row_at(s))
+
+        def stage(hh):
+            @pl.when((s >= in_lag[hh]) & (s < rows + in_lag[hh]))
+            def _():
+                inward(hh, row_at(s - in_lag[hh]))
+
+            @pl.when((s >= out_lag[hh]) & (s < rows + out_lag[hh]))
+            def _():
+                outward(hh, row_at(s - out_lag[hh]))
+
+        each_stage(stage)
         return carry
 
-    lax.fori_loop(0, rows, step, 0)
-
-    def rest(s, carry):
-        outward(row_at(s))
-        return carry
-
-    lax.fori_loop(rows - OUT_LAG, rows, rest, 0)
+    lax.fori_loop(0, rows + max(in_lag + out_lag), step, 0)
 
     for k in range(4):
         @pl.when(has[k])
@@ -529,7 +528,7 @@
     side = per * (n // 2)
     f32 = jnp.float32
     coef, send_tab, take_tab, rank = pl.pallas_call(
-        functools.partial(plan_kernel, n, per, False),
+        functools.partial(plan_kernel, n, per),
         out_shape=(
             jax.ShapeDtypeStruct((per, 3), f32),
             jax.ShapeDtypeStruct((side, side), f32),
@@ -540,35 +539,46 @@
         out_specs=(smem(),) * 4,
         name="plan",
     )(switch_mask, switch_cost, coef_table, mode_coef)
-    slots = side
     piece = (planes, cols, lanes)
     dma = pltpu.SemaphoreType.DMA
-    out = pl.pallas_call(
-        functools.partial(section_kernel, n, gx_count, gy_count, slots),
-        out_shape=jax.ShapeDtypeStruct((per, rows, cols * planes, lanes), f32),
-        in_specs=[smem()] * 3 + [pl.BlockSpec(memory_space=pl.ANY)],
-        out_specs=pl.BlockSpec(memory_space=pltpu.VMEM),
-        scratch_shapes=[
-            pltpu.VMEM((per, rows, cols * depth, lanes), f32),
-            pltpu.VMEM((planes, per, rows + 2 * REACH, cols + 2 * PAD, lanes), f32),
-            pltpu.VMEM((rows, per) + piece, f32),
-            pltpu.VMEM((rows, max(side - per, 1)) + piece, f32),
-            pltpu.VMEM((rows, side) + piece, f32),
-            pltpu.VMEM((rows, slots) + piece, f32),
-            pltpu.VMEM((rows, max(side - per, 1)) + piece, f32),
-            dma((per,)),
-            dma((4,)),
-            dma((4,)),
-            dma((rows, 2)),
-            dma((rows, 2)),
-            dma((rows,)),
-            dma((rows,)),
-        ],
-        compiler_params=pltpu.CompilerParams(
-            collective_id=0, has_side_effects=True, vmem_limit_bytes=58 * 1024 * 1024
-        ),
-        name="section",
-    )(coef, send_tab, take_tab, values.reshape(per, rows, cols * depth, lanes))
+    def section_with(slots, number):
+        return pl.pallas_call(
+            functools.partial(section_kernel, n, gx_count, gy_count, slots),
+            out_shape=jax.ShapeDtypeStruct((per, rows, cols * planes, lanes), f32),
+            in_specs=[smem()] * 3 + [pl.BlockSpec(memory_space=pl.ANY)],
+            out_specs=pl.BlockSpec(memory_space=pltpu.VMEM),
+            scratch_shapes=[
+                pltpu.VMEM((per, rows, cols * depth, lanes), f32),
+                pltpu.VMEM((planes, per, rows + 2 * REACH, cols + 2 * PAD, lanes), f32),
+                pltpu.VMEM((rows, per) + piece, f32),
+                pltpu.VMEM((rows, max(side - per, 1)) + piece, f32),
+                pltpu.VMEM((rows, side) + piece, f32),
+                pltpu.VMEM((rows, slots) + piece, f32),
+                pltpu.VMEM((rows, max(side - per, 1)) + piece, f32),
+                dma((per,)),
+                dma((4,)),
+                dma((4,)),
+                dma((rows, 2)),
+                dma((rows, 2)),
+                dma((rows,)),
+                dma((rows,)),
+            ],
+            compiler_params=pltpu.CompilerParams(
+                collective_id=number, has_side_effects=True, vmem_limit_bytes=58 * 1024 * 1024
+            ),
+            name="section",
+        )
+
+    sizes = sorted({max(side // 2, 1), max(3 * side // 4, 1), side})
+    pick = sum((rank[0] > size).astype(jnp.int32) for size in sizes[:-1])
+    out = lax.switch(
+        pick,
+        [section_with(size, number) for number, size in enumerate(sizes)],
+        coef,
+        send_tab,
+        take_tab,
+        values.reshape(per, rows, cols * depth, lanes),
+    )
     return out.reshape(per, rows, cols, planes, lanes)
 
 

time: 111 us -> 83.7 us (0.75)
  Pallas kernels: 108 us -> 81 us
  local copies, waits for them, and re-layouts: 2.71 us -> 1.17 us
  between operations: 0.02 us -> 1.32 us
    pallas_call x2, Pallas kernels: 108 us -> 81 us  [the longest x1 78.8 us: shards(): lax.switch(pick, [section_with(size, number) for number, size in enumerat...]
    unnamed x1, local copies, waits for them, and re-layouts: 2.71 us -> 1.17 us
where the time goes in v2:
time: 83.7 us; the launch traced here: 83.5 us
  Pallas kernels  81 us (97%)
  between operations  1.32 us (2%)
  local copies, waits for them, and re-layouts  1.17 us (1%)
    pallas_call x1, Pallas kernels, shards(): lax.switch(pick, [section_with(size, number) for number, size in enumerat...  78.8 us
    pallas_call x1, Pallas kernels, shards(): pl.pallas_call(functools.partial(plan_kernel, n, per), out_shape=(jax.Sha...  2.21 us

profile of v2, /device:TPU:0, one launch (start us, length us, event | category | flops | bytes accessed | tf_op | source)
XLA Modules:
  0.0 83.5 jit_solution(16565029714718362348)
XLA Ops:
  0.0 2.2 %plan.1 = (f32[2,3]{1,0:T(2,128)S(1)}, f32[4,4]{1,0:T(4,128)S(1)}, f32[6,10]{1,0:T(8,128)S(1)}, s32[1]{0:T(128)}) custom-call(s32[8,8]{1,0:T(8,128)} %mask.1, f32[8,8]{1,0:T(8,128)} %cost.1, f32[3,4]{1,0:T(4,128)} %table.1, s32[2]{0:T(128)} %kinds.1), custom_call_target="tpu_custom_call" | custom-call | tf_op jit(solution)/shard_map/plan/pallas_call | solution.py:530
  3.5 78.8 %conditional.1 = (f32[2,10,80,2,128]{4,3,2,1,0:T(2,128)S(1)}) conditional(s32[]{:T(128)} %bitcast.3, (f32[2,3]{1,0:T(2,128)S(1)}, f32[4,4]{1,0:T(4,128)S(1)}, f32[6,10]{1,0:T(8,128)S(1)}, f32[2,10,640,128]{3,2,1,0:T(8,128)}) %tuple.24, (f32[2,3]{1,0:T(2,128)S(1)}, f32[4,4]{1,0:T(4,128)S(1)}, f32[6,10]{1,0:T(8,128)S(1)}, ...), branch_computations={%region_0.0_spmd, %region_1.0_spmd, %region_2.0_spmd} | conditional | bytes 8 | solution.py:574
  3.5 78.8 %section.4 = f32[2,10,160,128]{3,2,1,0:T(8,128)S(1)} custom-call(f32[2,3]{1,0:T(2,128)S(1)} %get-tuple-element.38.coef, f32[4,4]{1,0:T(4,128)S(1)} %get-tuple-element.39.send_tab, f32[6,10]{1,0:T(8,128)S(1)} %get-tuple-element.40.take_tab, f32[2,10,640,128]{3,2,1,0:T(8,128)} %get-tuple-element.41.vals_hbm), custom_call_target="tpu_custom_call" | custom-call | tf_op jit(solution)/shard_map/cond/branch_1_fun/section/pallas_call | solution.py:574
  82.4 1.2 %copy.13 = f32[2,10,80,2,128]{4,3,2,1,0:T(2,128)} copy(f32[2,10,80,2,128]{4,3,2,1,0:T(2,128)S(1)} %get-tuple-element.54) | data formatting | bytes 3276800
